TPU v7x, 32 devices: a whole 2x2x4 slice. The times are simulated.
32 devices in a mesh: band: 8 (over y, x, core), head: 4 (over z).
Axes of the slice: x: 2, y: 2, z: 4, core: 2. Of those that a mesh axis runs over, the one named last changes fastest.
Arguments:
- queries: bfloat16 [1024, 1536], P('band', 'head'), as said below
- keys: bfloat16 [1024, 1536], P('band', 'head'), as said below
- values: bfloat16 [1024, 1536], P('band', 'head'), may hold values from -6 to 6
- d_out: bfloat16 [1024, 1536], P('band', 'head'), may hold values from -6 to 6
- gain: float32 [1536], P('head'), may hold values from 0.1 to 1.9
- blocks_on: int32 [8, 4], P('band'), may hold values 0 or 1
Outputs:
- out: bfloat16 [1024, 1536], P('band', 'head')
- d_queries: bfloat16 [1024, 1536], P('band', 'head')
- d_keys: bfloat16 [1024, 1536], P('band', 'head')
- d_values: bfloat16 [1024, 1536], P('band', 'head')
Inputs may be any that keep to these rules, and one draw needn't show every extreme that they name: `queries`: entries lie within -180 to 180. `keys`: entries lie within -6 to 6.
All inputs are finite; a program needn't handle non-finite values. No bound on the sum of `blocks_on` on one device may be relied on, other than what follows from the above.
Results may differ from a plain program's by a relative error of at most 0.0063.
Values may be sent and summed in bfloat16 or wider, within the bound.
No kernel may reach another device: no remote copies, remote signals or barrier semaphores. Data moves between devices by JAX's collectives and lax.ppermute only.
A program may use at most 64 MiB of HBM per device.

v0:
```python
import jax
import jax.numpy as jnp
from jax import lax
from jax.sharding import PartitionSpec as P

HEAD_DIM = 128


NEG = -1e30
EPS = 1e-06


def from_behind(array, axis, by):
    devices = lax.axis_size(axis)
    pairs = [(i, i + by) for i in range(devices) if 0 <= i + by < devices]
    return lax.ppermute(array, axis, pairs)


def row_pairs_matrix(left, right):
    return lax.dot_general(
        left, right, (((1,), (1,)), ((), ())), preferred_element_type=jnp.float32
    )


def cols_by_cols(left, right):
    return lax.dot_general(
        left, right, (((0,), (0,)), ((), ())), preferred_element_type=jnp.float32
    )


def product(left, right):
    return jnp.dot(left, right, preferred_element_type=jnp.float32)


def one_head(matrix, head_index):
    return matrix[:, head_index * HEAD_DIM : (head_index + 1) * HEAD_DIM]


def local(queries, keys, values, d_out, gain, blocks_on):
    row_count = queries.shape[0]
    heads_here = queries.shape[1] // HEAD_DIM
    blocks = lax.axis_size("band")
    spacing = blocks // 8
    block_offsets = [-2 * spacing, -spacing, spacing, 2 * spacing]
    position = lax.axis_index("band")
    scaling = HEAD_DIM ** (-0.5)
    full_width = queries.shape[1] * lax.axis_size("head")
    key_value = jnp.stack([keys, values])
    reached = [key_value]
    allowed = [jnp.ones((), jnp.bool_)]
    for slot_index, offset in enumerate(block_offsets):
        reached.append(from_behind(key_value, "band", -offset))
        target = position + offset
        allowed.append((target >= 0) & (target < blocks) & (blocks_on[0, slot_index] == 1))
    gathered = jnp.concatenate(reached, axis=1)
    key_all = gathered[0]
    value_all = gathered[1]
    column_ok = jnp.repeat(jnp.stack(allowed), row_count)

    def scores(head_index):
        raw_score = (
            row_pairs_matrix(one_head(queries, head_index), one_head(key_all, head_index)) * scaling
        )
        return jnp.where(column_ok[None, :], raw_score, NEG)

    peaks, totals, pieces = ([], [], [])
    for head_index in range(heads_here):
        score = scores(head_index)
        peak = jnp.max(score, axis=1)
        exponent = jnp.exp(score - peak[:, None])
        total = jnp.sum(exponent, axis=1)
        weight_probs = (exponent / total[:, None]).astype(jnp.bfloat16)
        pieces.append(product(weight_probs, one_head(value_all, head_index)).astype(jnp.bfloat16))
        peaks.append(peak)
        totals.append(total)
    attention = jnp.concatenate(pieces, axis=1)
    attention_wide = attention.astype(jnp.float32)
    square_sum = lax.psum(jnp.sum(attention_wide * attention_wide, axis=1), "head")
    inverse = lax.rsqrt(square_sum / full_width + EPS)
    out = (attention_wide * inverse[:, None] * gain).astype(jnp.bfloat16)
    gradient_pass = d_out.astype(jnp.float32) * gain
    along = lax.psum(jnp.sum(gradient_pass * attention_wide, axis=1), "head")
    d_attn = (
        inverse[:, None] * gradient_pass
        - attention_wide * (inverse**3 * along / full_width)[:, None]
    ).astype(jnp.bfloat16)
    deltas = [
        jnp.sum(
            one_head(d_attn, head_index).astype(jnp.float32) * one_head(attention_wide, head_index),
            axis=1,
        )
        for head_index in range(heads_here)
    ]
    query_parts, key_parts, value_parts = ([], [], [])
    for head_index in range(heads_here):
        score = scores(head_index)
        probs = jnp.exp(score - peaks[head_index][:, None]) / totals[head_index][:, None]
        upstream = one_head(d_attn, head_index)
        d_weights = row_pairs_matrix(upstream, one_head(value_all, head_index))
        d_score = (probs * (d_weights - deltas[head_index][:, None])).astype(jnp.bfloat16)
        query_parts.append(product(d_score, one_head(key_all, head_index)) * scaling)
        weight_probs = probs.astype(jnp.bfloat16)
        key_parts.append(cols_by_cols(d_score, one_head(queries, head_index)) * scaling)
        value_parts.append(cols_by_cols(weight_probs, upstream))
    d_queries = jnp.concatenate(query_parts, axis=1).astype(jnp.bfloat16)
    stacked_grads = jnp.stack(
        [jnp.concatenate(key_parts, axis=1), jnp.concatenate(value_parts, axis=1)]
    )
    summed = stacked_grads[:, :row_count]
    for slot_index, offset in enumerate(block_offsets):
        outgoing = stacked_grads[
            :, (slot_index + 1) * row_count : (slot_index + 2) * row_count
        ].astype(jnp.bfloat16)
        arrived = from_behind(outgoing, "band", offset)
        summed = summed + arrived.astype(jnp.float32)
    d_keys = summed[0].astype(jnp.bfloat16)
    d_values = summed[1].astype(jnp.bfloat16)
    return (out, d_queries, d_keys, d_values)


def solution(mesh):
    in_specs = (
        P("band", "head"),
        P("band", "head"),
        P("band", "head"),
        P("band", "head"),
        P("head"),
        P("band", None),
    )
    out_specs = (P("band", "head"), P("band", "head"), P("band", "head"), P("band", "head"))
    return jax.shard_map(local, mesh=mesh, in_specs=in_specs, out_specs=out_specs, check_vma=False)
```

profile of v0, /device:TPU:1, one launch (start us, length us, event | category | flops | bytes accessed | tf_op | source)
XLA Modules:
  0.0 59.1 jit_solution(17410145999609691004)
XLA Ops:
  0.6 1.0 %pad_maximum_fusion.1 = (bf16[2,128,384]{2,1,0:T(8,128)(2,1)S(1)}, bf16[2,640,384]{2,1,0:T(8,128)(2,1)S(1)}) fusion(bf16[1,128,384]{2,1,0:T(8,128)(2,1)} %bitcast.45, bf16[1,128,384]{2,1,0:T(8,128)(2,1)} %bitcast.46), kind=kLoop, calls=%fused_computation.53 | loop fusion | flops 393215 | bytes 589824 | tf_op jit(solution)/shard_map/stack | solution.py:48
  1.6 2.0 %collective-permute-start.2 = (bf16[2,128,384]{2,1,0:T(8,128)(2,1)S(1)}, bf16[2,128,384]{2,1,0:T(8,128)(2,1)S(1)}, u32[]{:S(2)}, u32[]{:S(2)}) collective-permute-start(bf16[2,128,384]{2,1,0:T(8,128)(2,1)S(1)} %get-tuple-element.23), channel_id=1, source_target_pairs={{4,0},{8,4},{12,8},{16,12},{20,16},{24,20},{28,24},{5,1},{9,5},{13... | collective-permute-start | bytes 589832 | tf_op jit(solution)/shard_map/ppermute | solution.py:16
  3.6 4.5 %collective-permute-start.1 = (bf16[2,128,384]{2,1,0:T(8,128)(2,1)S(1)}, bf16[2,128,384]{2,1,0:T(8,128)(2,1)S(1)}, u32[]{:S(2)}, u32[]{:S(2)}) collective-permute-start(bf16[2,128,384]{2,1,0:T(8,128)(2,1)S(1)} %get-tuple-element.23), channel_id=1, source_target_pairs={{0,4},{4,8},{8,12},{12,16},{16,20},{20,24},{24,28},{1,5},{5,9},{9,... | collective-permute-start | bytes 589832 | tf_op jit(solution)/shard_map/ppermute | solution.py:16
  8.1 4.0 %collective-permute-start = (bf16[2,128,384]{2,1,0:T(8,128)(2,1)S(1)}, bf16[2,128,384]{2,1,0:T(8,128)(2,1)S(1)}, u32[]{:S(2)}, u32[]{:S(2)}) collective-permute-start(bf16[2,128,384]{2,1,0:T(8,128)(2,1)S(1)} %get-tuple-element.23), channel_id=1, source_target_pairs={{0,8},{4,12},{8,16},{12,20},{16,24},{20,28},{1,9},{5,13},{9,17},{1... | collective-permute-start | bytes 589832 | tf_op jit(solution)/shard_map/ppermute | solution.py:16
  12.1 1.3 %collective-permute-start.3 = (bf16[2,128,384]{2,1,0:T(8,128)(2,1)S(1)}, bf16[2,128,384]{2,1,0:T(8,128)(2,1)S(1)}, u32[]{:S(2)}, u32[]{:S(2)}) collective-permute-start(bf16[2,128,384]{2,1,0:T(8,128)(2,1)S(1)} %get-tuple-element.23), channel_id=1, source_target_pairs={{8,0},{12,4},{16,8},{20,12},{24,16},{28,20},{9,1},{13,5},{17,9},{2... | collective-permute-start | bytes 589832 | tf_op jit(solution)/shard_map/ppermute | solution.py:16
  13.4 1.4 %fusion.59 = (s32[1,1]{1,0:T(1,128)}, s32[1,1]{1,0:T(1,128)}, s32[1,1]{1,0:T(1,128)}, s32[1,1]{1,0:T(1,128)}) fusion(s32[1,4]{1,0:T(1,128)} %param.11), kind=kLoop, calls=%fused_computation.108 | loop fusion | bytes 32 | tf_op jit(solution)/shard_map/slice | solution.py:54
  17.6 1.0 %copy.10 = bf16[128,384]{0,1:T(8,128)(2,1)S(1)} copy(bf16[128,384]{1,0:T(8,128)(2,1)} %param.9) | data formatting | bytes 196608 | tf_op args[3]
  18.7 3.1 %collective-permute-done.3 = bf16[2,128,384]{2,1,0:T(8,128)(2,1)S(1)} collective-permute-done((bf16[2,128,384]{2,1,0:T(8,128)(2,1)S(1)}, bf16[2,128,384]{2,1,0:T(8,128)(2,1)S(1)}, u32[]{:S(2)}, u32[]{:S(2)}) %collective-permute-start.3) | collective-permute-done | bytes 196640 | tf_op jit(solution)/shard_map/ppermute | solution.py:16
  22.0 0.8 %copy-done = bf16[128,384]{1,0:T(8,128)(2,1)S(1)} copy-done((bf16[128,384]{1,0:T(8,128)(2,1)S(1)}, bf16[128,384]{1,0:T(8,128)(2,1)}, u32[]{:S(2)}) %copy-start) | copy-done | bytes 98328
  23.0 0.3 fusion.61
  25.1 9.9 %all-reduce = (f32[128]{0:T(128)S(1)}, f32[128]{0:T(128)S(1)}) all-reduce(f32[128]{0:T(128)S(1)} %get-tuple-element.12, f32[128]{0:T(128)S(1)} %get-tuple-element.11), channel_id=1, replica_groups=mesh['band'=8,'head'=4] {'head'}, use_global_device_ids=true, to_apply=%region_7.8 | all-reduce | flops 256 | bytes 2048 | tf_op jit(solution)/shard_map/psum | solution.py:78
  35.4 0.3 fusion.11
  36.1 0.3 fusion.10
  37.8 0.8 %fusion.58 = (bf16[2,128,384]{2,1,0:T(8,128)(2,1)}, bf16[2,128,384]{2,1,0:T(8,128)(2,1)}, bf16[2,128,384]{2,1,0:T(8,128)(2,1)S(1)}, bf16[2,128,384]{2,1,0:T(8,128)(2,1)S(1)}) fusion(bf16[2,640,384]{2,1,0:T(8,128)(2,1)S(1)} %fusion), kind=kLoop, calls=%fused_computation.107 | loop fusion | bytes 1572864 | tf_op jit(solution)/shard_map/slice | solution.py:111
  38.6 1.3 %collective-permute-start.4 = (bf16[2,128,384]{2,1,0:T(8,128)(2,1)}, bf16[2,128,384]{2,1,0:T(8,128)(2,1)S(1)}, u32[]{:S(2)}, u32[]{:S(2)}) collective-permute-start(bf16[2,128,384]{2,1,0:T(8,128)(2,1)} %get-tuple-element.15), channel_id=1, source_target_pairs={{8,0},{12,4},{16,8},{20,12},{24,16},{28,20},{9,1},{13,5},{17,9},{2... | collective-permute-start | bytes 589832 | tf_op jit(solution)/shard_map/ppermute | solution.py:16
  39.9 4.0 %collective-permute-start.7 = (bf16[2,128,384]{2,1,0:T(8,128)(2,1)}, bf16[2,128,384]{2,1,0:T(8,128)(2,1)S(1)}, u32[]{:S(2)}, u32[]{:S(2)}) collective-permute-start(bf16[2,128,384]{2,1,0:T(8,128)(2,1)} %get-tuple-element.16), channel_id=1, source_target_pairs={{0,8},{4,12},{8,16},{12,20},{16,24},{20,28},{1,9},{5,13},{9,17},{1... | collective-permute-start | bytes 589832 | tf_op jit(solution)/shard_map/ppermute | solution.py:16
  43.9 6.3 %collective-permute-start.6 = (bf16[2,128,384]{2,1,0:T(8,128)(2,1)S(1)}, bf16[2,128,384]{2,1,0:T(8,128)(2,1)}, u32[]{:S(2)}, u32[]{:S(2)}) collective-permute-start(bf16[2,128,384]{2,1,0:T(8,128)(2,1)S(1)} %get-tuple-element.17), channel_id=1, source_target_pairs={{0,4},{4,8},{8,12},{12,16},{16,20},{20,24},{24,28},{1,5},{5,9},{9,... | collective-permute-start | bytes 589832 | tf_op jit(solution)/shard_map/ppermute | solution.py:16
  50.2 1.9 %collective-permute-start.5 = (bf16[2,128,384]{2,1,0:T(8,128)(2,1)S(1)}, bf16[2,128,384]{2,1,0:T(8,128)(2,1)}, u32[]{:S(2)}, u32[]{:S(2)}) collective-permute-start(bf16[2,128,384]{2,1,0:T(8,128)(2,1)S(1)} %get-tuple-element.18), channel_id=1, source_target_pairs={{4,0},{8,4},{12,8},{16,12},{20,16},{24,20},{28,24},{5,1},{9,5},{13... | collective-permute-start | bytes 589832 | tf_op jit(solution)/shard_map/ppermute | solution.py:16
  52.1 0.3 fusion.12
  52.4 0.8 %copy.20 = bf16[128,384]{1,0:T(8,128)(2,1)} copy(bf16[128,384]{0,1:T(8,128)(2,1)S(1)} %get-tuple-element.26) | data formatting | bytes 196608
  53.2 0.8 %copy.21 = bf16[128,384]{1,0:T(8,128)(2,1)} copy(bf16[128,384]{0,1:T(8,128)(2,1)S(1)} %pad_maximum_fusion.3) | data formatting | bytes 196608
  53.9 3.4 %collective-permute-done.5 = bf16[2,128,384]{2,1,0:T(8,128)(2,1)} collective-permute-done((bf16[2,128,384]{2,1,0:T(8,128)(2,1)S(1)}, bf16[2,128,384]{2,1,0:T(8,128)(2,1)}, u32[]{:S(2)}, u32[]{:S(2)}) %collective-permute-start.5) | collective-permute-done | bytes 196640 | tf_op jit(solution)/shard_map/ppermute | solution.py:16
  57.3 1.1 %fusion.18 = bf16[2,128,384]{2,1,0:T(8,128)(2,1)S(1)} fusion(f32[1,640,384]{2,1,0:T(8,128)S(1)} %get-tuple-element.39, f32[1,640,384]{2,1,0:T(8,128)S(1)} %get-tuple-element.40, bf16[2,128,384]{2,1,0:T(8,128)(2,1)S(1)} %collective-permute-done.7, bf16[2,128,384]{2,1,0:T(8,128)(2,1)} %collective-permute-done.6, ...), kind=kLoop, calls=%fused_computation.40 | loop fusion | flops 983040 | bytes 2949120 | tf_op jit(solution)/shard_map/convert.1
  58.4 0.7 %slice_bitcast_fusion.2 = (bf16[128,384]{1,0:T(8,128)(2,1)}, bf16[128,384]{1,0:T(8,128)(2,1)}) fusion(bf16[2,128,384]{2,1,0:T(8,128)(2,1)S(1)} %fusion.18), kind=kLoop, calls=%fused_computation.71 | loop fusion | bytes 393216 | tf_op jit(solution)/shard_map/convert_element_type | solution.py:117
  (44 shorter events, 4.6 us)
Async XLA Ops:
  1.6 17.1 %collective-permute-start.2 = (bf16[2,128,384]{2,1,0:T(8,128)(2,1)S(1)}, bf16[2,128,384]{2,1,0:T(8,128)(2,1)S(1)}, u32[]{:S(2)}, u32[]{:S(2)}) collective-permute-start(bf16[2,128,384]{2,1,0:T(8,128)(2,1)S(1)} %get-tuple-element.23), channel_id=1, source_target_pairs={{4,0},{8,4},{12,8},{16,12},{20,16},{24,20},{28,24},{5,1},{9,5},{13... | collective-permute-start | bytes 589832 | tf_op jit(solution)/shard_map/ppermute | solution.py:16
  3.6 15.1 %collective-permute-start.1 = (bf16[2,128,384]{2,1,0:T(8,128)(2,1)S(1)}, bf16[2,128,384]{2,1,0:T(8,128)(2,1)S(1)}, u32[]{:S(2)}, u32[]{:S(2)}) collective-permute-start(bf16[2,128,384]{2,1,0:T(8,128)(2,1)S(1)} %get-tuple-element.23), channel_id=1, source_target_pairs={{0,4},{4,8},{8,12},{12,16},{16,20},{20,24},{24,28},{1,5},{5,9},{9,... | collective-permute-start | bytes 589832 | tf_op jit(solution)/shard_map/ppermute | solution.py:16
  8.1 10.5 %collective-permute-start = (bf16[2,128,384]{2,1,0:T(8,128)(2,1)S(1)}, bf16[2,128,384]{2,1,0:T(8,128)(2,1)S(1)}, u32[]{:S(2)}, u32[]{:S(2)}) collective-permute-start(bf16[2,128,384]{2,1,0:T(8,128)(2,1)S(1)} %get-tuple-element.23), channel_id=1, source_target_pairs={{0,8},{4,12},{8,16},{12,20},{16,24},{20,28},{1,9},{5,13},{9,17},{1... | collective-permute-start | bytes 589832 | tf_op jit(solution)/shard_map/ppermute | solution.py:16
  12.1 9.7 %collective-permute-start.3 = (bf16[2,128,384]{2,1,0:T(8,128)(2,1)S(1)}, bf16[2,128,384]{2,1,0:T(8,128)(2,1)S(1)}, u32[]{:S(2)}, u32[]{:S(2)}) collective-permute-start(bf16[2,128,384]{2,1,0:T(8,128)(2,1)S(1)} %get-tuple-element.23), channel_id=1, source_target_pairs={{8,0},{12,4},{16,8},{20,12},{24,16},{28,20},{9,1},{13,5},{17,9},{2... | collective-permute-start | bytes 589832 | tf_op jit(solution)/shard_map/ppermute | solution.py:16
  21.8 0.9 %copy-start = (bf16[128,384]{1,0:T(8,128)(2,1)S(1)}, bf16[128,384]{1,0:T(8,128)(2,1)}, u32[]{:S(2)}) copy-start(bf16[128,384]{1,0:T(8,128)(2,1)} %param.6) | copy-start | bytes 294916
  24.2 0.8 %copy-start.1 = (f32[384]{0:T(512)S(1)}, f32[384]{0:T(512)}, u32[]{:S(2)}) copy-start(f32[384]{0:T(512)} %param.10) | copy-start | bytes 4612
  38.6 15.3 %collective-permute-start.4 = (bf16[2,128,384]{2,1,0:T(8,128)(2,1)}, bf16[2,128,384]{2,1,0:T(8,128)(2,1)S(1)}, u32[]{:S(2)}, u32[]{:S(2)}) collective-permute-start(bf16[2,128,384]{2,1,0:T(8,128)(2,1)} %get-tuple-element.15), channel_id=1, source_target_pairs={{8,0},{12,4},{16,8},{20,12},{24,16},{28,20},{9,1},{13,5},{17,9},{2... | collective-permute-start | bytes 589832 | tf_op jit(solution)/shard_map/ppermute | solution.py:16
  39.9 14.0 %collective-permute-start.7 = (bf16[2,128,384]{2,1,0:T(8,128)(2,1)}, bf16[2,128,384]{2,1,0:T(8,128)(2,1)S(1)}, u32[]{:S(2)}, u32[]{:S(2)}) collective-permute-start(bf16[2,128,384]{2,1,0:T(8,128)(2,1)} %get-tuple-element.16), channel_id=1, source_target_pairs={{0,8},{4,12},{8,16},{12,20},{16,24},{20,28},{1,9},{5,13},{9,17},{1... | collective-permute-start | bytes 589832 | tf_op jit(solution)/shard_map/ppermute | solution.py:16
  43.9 10.0 %collective-permute-start.6 = (bf16[2,128,384]{2,1,0:T(8,128)(2,1)S(1)}, bf16[2,128,384]{2,1,0:T(8,128)(2,1)}, u32[]{:S(2)}, u32[]{:S(2)}) collective-permute-start(bf16[2,128,384]{2,1,0:T(8,128)(2,1)S(1)} %get-tuple-element.17), channel_id=1, source_target_pairs={{0,4},{4,8},{8,12},{12,16},{16,20},{20,24},{24,28},{1,5},{5,9},{9,... | collective-permute-start | bytes 589832 | tf_op jit(solution)/shard_map/ppermute | solution.py:16
  50.2 7.1 %collective-permute-start.5 = (bf16[2,128,384]{2,1,0:T(8,128)(2,1)S(1)}, bf16[2,128,384]{2,1,0:T(8,128)(2,1)}, u32[]{:S(2)}, u32[]{:S(2)}) collective-permute-start(bf16[2,128,384]{2,1,0:T(8,128)(2,1)S(1)} %get-tuple-element.18), channel_id=1, source_target_pairs={{4,0},{8,4},{12,8},{16,12},{20,16},{24,20},{28,24},{5,1},{9,5},{13... | collective-permute-start | bytes 589832 | tf_op jit(solution)/shard_map/ppermute | solution.py:16
where the time goes:
time: 59.6 us; the launch traced here: 59.1 us
  starting transfers between devices  25.2 us (42%)
  blocking collectives  9.94 us (17%)
  local copies, waits for them, and re-layouts  6.63 us (11%)
  waiting for transfers between devices  6.43 us (11%)
  matrix products  4.13 us (7%)
  between operations  3.57 us (6%)
  other arithmetic  3.26 us (5%)
    ppermute x8, starting transfers between devices, from_behind(): return lax.ppermute(array, axis, pairs)  25.2 us
    psum x1, blocking collectives, local(): lax.psum(jnp.sum(attention_wide * attention_wide, axis=1), 'head')  9.94 us
    ppermute x8, waiting for transfers between devices, from_behind(): return lax.ppermute(array, axis, pairs)  6.43 us
    unnamed x10, local copies, waits for them, and re-layouts  3.4 us
    dot_general x6, matrix products, product(): return jnp.dot(left, right, preferred_element_type=jnp.float32)  1.61 us
    slice x1, local copies, waits for them, and re-layouts, local(): blocks_on[0, slot_index] == 1  1.4 us
    dot_general x6, matrix products, row_pairs_matrix(): lax.dot_general(left, right, (((1,), (1,)), ((), ())), preferred_element_...  1.38 us
    another operation x2, other arithmetic  1.3 us
  transfers between devices with their start and end apart: 8, of which 2 were waited for; matrix products, arithmetic and copies ran while one was open for 8% of the time, Pallas kernels for 0%

commit v1 on v0

v1 whole, which is shorter than its diff:
```python
import functools

import jax
import jax.numpy as jnp
from jax import lax
from jax.experimental import pallas as pl
from jax.experimental.pallas import tpu as pltpu
from jax.sharding import PartitionSpec as P

HEAD_DIM = 128
NEG = -1e30
EPS = 1e-06
SCALING = HEAD_DIM ** (-0.5)
STAT_ROWS = 16
F32 = jnp.float32
BF16 = jnp.bfloat16
VMEM_BYTES = 24 * 1024 * 1024


def matmul_nt(left, right):
    return lax.dot_general(left, right, (((1,), (1,)), ((), ())), preferred_element_type=F32)


def matmul(left, right):
    return jnp.dot(left, right, preferred_element_type=F32)


def head_slice(h):
    return slice(h * HEAD_DIM, (h + 1) * HEAD_DIM)


def matmul_tn(left, right):
    return lax.dot_general(left, right, (((0,), (0,)), ((), ())), preferred_element_type=F32)


def stack_rows(lines, shape):
    sub = lax.broadcasted_iota(jnp.int32, shape, 0)
    packed = jnp.zeros(shape, F32)
    for i, line in enumerate(lines):
        packed = jnp.where(sub == i, line, packed)
    return packed


def three_parts(row):
    high = row.astype(BF16).astype(F32)
    mid = (row - high).astype(BF16).astype(F32)
    low = row - high - mid
    return [high, mid, low]


def place(spacing):
    step = lax.div(lax.axis_index("band"), spacing)
    return lax.rem(step, 2) == 0, lax.rem(lax.div(step, 2), 2) == 0


def flag_lines(flags_ref, spacing, blocks, shape):
    position = lax.axis_index("band")
    raw, inside = [], []
    for slot, offset in enumerate((-2 * spacing, -spacing, spacing, 2 * spacing)):
        target = position + offset
        on = flags_ref[0, slot] == 1
        raw.append(jnp.where(on, 1.0, 0.0))
        inside.append(jnp.where(on & (target >= 0) & (target < blocks), 1.0, 0.0))
    m2, m1, p1, p2 = inside
    first, even = place(spacing)
    attended = [
        jnp.where(first, p1, m1),
        jnp.where(even, p2, m2),
        jnp.where(even, m2, p2),
        jnp.where(first, m1, p1),
    ]
    return stack_rows(raw + attended, shape)


def raw_scores(q, keys, flags):
    scores = matmul_nt(jnp.concatenate(keys, axis=0), q) * SCALING
    n = keys[0].shape[0]
    parts = [scores[j * n : (j + 1) * n] for j in range(len(keys))]
    return [s if flag is None else jnp.where(flag > 0.5, s, NEG) for s, flag in zip(parts, flags)]


def top(scores):
    return jnp.max(functools.reduce(jnp.maximum, scores), axis=0, keepdims=True)


def total_of(exps):
    return jnp.sum(functools.reduce(jnp.add, exps), axis=0, keepdims=True)


def near_kernel(
    spacing, blocks, flags_ref, q_ref, g_ref, gain_ref, own, inner, partner,
    exps_ref, lines_ref, grad_ref, on_ref,
):
    rows = q_ref.shape[0]
    heads = q_ref.shape[1] // HEAD_DIM
    on_ref[...] = flag_lines(flags_ref, spacing, blocks, on_ref.shape)
    flags = [None, on_ref[4:5], on_ref[5:6]]
    held = [own, partner, inner]
    peaks, totals = [], []
    for h in range(heads):
        sl = head_slice(h)
        scores = raw_scores(q_ref[:, sl], [r[0, :, sl] for r in held], flags)
        peak = top(scores)
        exps = [jnp.exp(s - peak) for s in scores]
        peaks.append(peak)
        totals.append(total_of(exps))
        for j, e in enumerate(exps):
            at = (h * len(held) + j) * rows
            exps_ref[at : at + rows] = e
        grad_ref[sl] = (g_ref[:, sl].astype(F32) * gain_ref[:, sl]).T
    lines_ref[...] = stack_rows(peaks + totals, lines_ref.shape)


def far_kernel(
    q_ref, grad_ref, exps_ref, near_ref, on_ref, own, partner, inner, outer, fifth,
    attn_ref, stats_ref, sums_ref,
):
    heads = q_ref.shape[1] // HEAD_DIM
    near_rows = exps_ref.shape[0] // heads
    flags = [on_ref[6:7], on_ref[7:8]]
    held = [outer, fifth]
    peaks, inverse_totals = [], []
    square = along = 0.0
    for h in range(heads):
        sl = head_slice(h)
        scores = raw_scores(q_ref[:, sl], [r[0, :, sl] for r in held], flags)
        before = near_ref[h : h + 1]
        peak = jnp.maximum(before, top(scores))
        exps = [jnp.exp(s - peak) for s in scores]
        factor = jnp.exp(before - peak)
        inverse_total = 1.0 / (factor * near_ref[heads + h : heads + h + 1] + total_of(exps))
        near = exps_ref[h * near_rows : (h + 1) * near_rows] * (factor * inverse_total)
        weights = [near.astype(BF16)] + [(e * inverse_total).astype(BF16) for e in exps]
        values = [r[1, :, sl] for r in (own, partner, inner, outer, fifth)]
        attn = matmul_tn(jnp.concatenate(values, axis=0), jnp.concatenate(weights, axis=0)).astype(BF16)
        attn_ref[sl] = attn
        wide = attn.astype(F32)
        square = square + wide * wide
        along = along + grad_ref[sl] * wide
        peaks.append(peak)
        inverse_totals.append(inverse_total)
    stats_ref[...] = stack_rows(peaks + inverse_totals, stats_ref.shape)
    sums_ref[...] = stack_rows(
        [jnp.sum(square, axis=0, keepdims=True), jnp.sum(along, axis=0, keepdims=True)],
        sums_ref.shape,
    )


def message_kernel(width, n_parts, *refs):
    on_ref, attn_ref, grad_ref, stats_ref = refs[:4]
    part_refs = refs[4 : 4 + n_parts]
    msg_ref, lines_ref = refs[4 + n_parts :]
    width_here, rows = attn_ref.shape
    heads = width_here // HEAD_DIM
    sums = functools.reduce(jnp.add, [r[...] for r in part_refs])
    inverse = lax.rsqrt(sums[0:1] / width + EPS)
    second = inverse * inverse * inverse * sums[1:2] / width
    line = lambda kind, h: stats_ref[kind * heads + h : kind * heads + h + 1]
    deltas = []
    for h in range(heads):
        sl = head_slice(h)
        attn = attn_ref[sl].astype(F32)
        d_attn = (inverse * grad_ref[sl] - attn * second).astype(BF16)
        msg_ref[sl] = d_attn
        deltas.append(jnp.sum(d_attn.astype(F32) * attn, axis=0, keepdims=True))
    flags = [on_ref[slot : slot + 1] for slot in range(4)]
    for h in range(heads):
        sent = three_parts(line(0, h)) + three_parts(line(1, h)) + three_parts(deltas[h]) + flags
        at = width_here + h * STAT_ROWS
        msg_ref[at : at + STAT_ROWS] = stack_rows(sent, (STAT_ROWS, rows)).astype(BF16)
    lines_ref[...] = stack_rows(deltas + [inverse], lines_ref.shape)


def query_kernel(
    on_ref, q_ref, gain_ref, attn_ref, msg_ref, stats_ref, lines_ref,
    own, partner, inner, outer, fifth, out_ref, dq_ref,
):
    rows = q_ref.shape[0]
    heads = q_ref.shape[1] // HEAD_DIM
    flags = [None] + [on_ref[i : i + 1] for i in range(4, 8)]
    held = [own, partner, inner, outer, fifth]
    inverse = lines_ref[heads : heads + 1]
    for h in range(heads):
        sl = head_slice(h)
        out_ref[:, sl] = ((attn_ref[sl].astype(F32) * inverse).T * gain_ref[:, sl]).astype(BF16)
        keys = [r[0, :, sl] for r in held]
        scores = raw_scores(q_ref[:, sl], keys, flags)
        peak = stats_ref[h : h + 1]
        inverse_total = stats_ref[heads + h : heads + h + 1]
        delta = lines_ref[h : h + 1]
        d_weights = matmul(jnp.concatenate([r[1, :, sl] for r in held], axis=0), msg_ref[sl])
        d_scores = [
            (
                jnp.exp(s - peak)
                * inverse_total
                * (d_weights[j * rows : (j + 1) * rows] - delta)
            ).astype(BF16)
            for j, s in enumerate(scores)
        ]
        dq = matmul_tn(jnp.concatenate(d_scores, axis=0), jnp.concatenate(keys, axis=0))
        dq_ref[:, sl] = (dq * SCALING).astype(BF16)


def key_parts(own, h, q_refs, m_refs, slots, spacing):
    sl = head_slice(h)
    rows, width_here = own.shape[1:]
    first, even = place(spacing)
    queries = jnp.concatenate([r[:, sl] for r in q_refs], axis=0)
    d_attn = jnp.concatenate([r[sl] for r in m_refs], axis=1)
    scores = matmul_nt(own[0, :, sl], queries) * SCALING
    d_weights = matmul(own[1, :, sl], d_attn)
    at = width_here + h * STAT_ROWS
    weights, d_scores = [], []
    for j, (m_ref, slot) in enumerate(zip(m_refs, slots)):
        stats = m_ref[at : at + STAT_ROWS].astype(F32)
        peak = stats[0:1] + stats[1:2] + stats[2:3]
        inverse_total = stats[3:4] + stats[4:5] + stats[5:6]
        delta = stats[6:7] + stats[7:8] + stats[8:9]
        score = scores[:, j * rows : (j + 1) * rows]
        if slot > 0:
            at_m2, at_m1, at_p1, at_p2 = [stats[9 + i : 10 + i] for i in range(4)]
            flag = [
                None,
                jnp.where(first, at_m1, at_p1),
                jnp.where(even, at_m2, at_p2),
                jnp.where(even, at_p2, at_m2),
                jnp.where(first, at_p1, at_m1),
            ][slot]
            score = jnp.where(flag > 0.5, score, NEG)
        weight = jnp.exp(score - peak) * inverse_total
        weights.append(weight.astype(BF16))
        d_scores.append((weight * (d_weights[:, j * rows : (j + 1) * rows] - delta)).astype(BF16))
    d_values = matmul_nt(jnp.concatenate(weights, axis=1), d_attn)
    return matmul(jnp.concatenate(d_scores, axis=1), queries), d_values


def near_key_kernel(spacing, own, q0, q1, q2, q3, m0, m1, m2, m3, dk_ref, dv_ref):
    for h in range(own.shape[2] // HEAD_DIM):
        dk_ref[:, head_slice(h)], dv_ref[:, head_slice(h)] = key_parts(
            own, h, [q0, q1, q2, q3], [m0, m1, m2, m3], (0, 1, 2, 3), spacing
        )


def far_key_kernel(spacing, own, dk_near, dv_near, q4, m4, dk_ref, dv_ref):
    for h in range(own.shape[2] // HEAD_DIM):
        sl = head_slice(h)
        dk, dv = key_parts(own, h, [q4], [m4], (4,), spacing)
        dk_ref[:, sl] = ((dk_near[:, sl] + dk) * SCALING).astype(BF16)
        dv_ref[:, sl] = (dv_near[:, sl] + dv).astype(BF16)


def call(kernel, name, out_shape, args, smem_first=False, cost=None):
    specs = [pl.BlockSpec(memory_space=pltpu.VMEM) for _ in args]
    if smem_first:
        specs[0] = pl.BlockSpec(memory_space=pltpu.SMEM)
    return pl.pallas_call(
        kernel,
        name=name,
        out_shape=out_shape,
        in_specs=specs,
        out_specs=jax.tree.map(lambda _: pl.BlockSpec(memory_space=pltpu.VMEM), out_shape),
        cost_estimate=cost,
        compiler_params=pltpu.CompilerParams(vmem_limit_bytes=VMEM_BYTES),
    )(*args)


def pairs_of(blocks, spacing):
    partner, inner, outer, relay = [], [], [], []
    for i in range(blocks):
        step = i // spacing
        partner.append((i, i + spacing if step % 2 == 0 else i - spacing))
        to = 2 * spacing if (step // 2) % 2 == 0 else -2 * spacing
        if 0 <= i + to < blocks:
            inner.append((i, i + to))
            if 0 <= i + 2 * to < blocks:
                relay.append((i, i + 2 * to))
        if 0 <= i - to < blocks:
            outer.append((i, i - to))
    return partner, inner, outer, relay


def head_sum_parts(sums, devices):
    parts = [sums]
    order = list(range(1, devices))
    for k in order[1:] + order[:1]:
        if devices & (devices - 1) == 0:
            pairs = [(i, i ^ k) for i in range(devices)]
        else:
            pairs = [(i, (i + k) % devices) for i in range(devices)]
        parts.append(lax.ppermute(sums, "head", pairs))
    return parts


def local(queries, keys, values, d_out, gain, blocks_on):
    rows, width_here = queries.shape
    blocks = lax.axis_size("band")
    head_devices = lax.axis_size("head")
    spacing = blocks // 8
    heads = width_here // HEAD_DIM
    width = width_here * head_devices
    gain = gain[None, :]
    partner_pairs, inner_pairs, outer_pairs, relay_pairs = pairs_of(blocks, spacing)
    first, even = place(spacing)

    def wide(lines, dtype=F32):
        return jax.ShapeDtypeStruct((lines, width_here), dtype)

    def narrow(lines, dtype=F32):
        return jax.ShapeDtypeStruct((lines, rows), dtype)

    def to_partner(array):
        return lax.ppermute(array, "band", partner_pairs)

    def swaps(array):
        return [lax.ppermute(array, "band", pairs) for pairs in (inner_pairs, outer_pairs)]

    def passed_on(inner, outer):
        return to_partner(lax.select(first == even, inner, outer))

    own = jnp.stack([keys, values])
    inner, outer = swaps(own)
    partner = to_partner(own)
    q_partner = to_partner(queries)
    exps, near_lines, grad, on = call(
        functools.partial(near_kernel, spacing, blocks),
        "near_attention",
        (narrow(3 * rows * heads), narrow(8), narrow(width_here), narrow(8)),
        (blocks_on, queries, d_out, gain, own, inner, partner),
        smem_first=True,
    )
    exps, q_partner, queries_late = lax.optimization_barrier((exps, q_partner, queries))
    exps, outer = lax.optimization_barrier((exps, outer))
    fifth = passed_on(inner, outer)
    q_inner = lax.ppermute(queries_late, "band", inner_pairs)
    attn, stats, sums = call(
        far_kernel,
        "far_attention",
        (narrow(width_here, BF16), narrow(8), narrow(8)),
        (queries, grad, exps, near_lines, on, own, partner, inner, outer, fifth),
    )
    attn, q_relayed = lax.optimization_barrier((attn, q_inner))
    q_outer = lax.ppermute(q_relayed, "band", relay_pairs)
    parts = head_sum_parts(sums, head_devices)
    q_inner, parts = lax.optimization_barrier((q_inner, parts))
    msg, lines = call(
        functools.partial(message_kernel, width, head_devices),
        "attention_gradient",
        (narrow(width_here + heads * STAT_ROWS, BF16), narrow(8)),
        (on, attn, grad, stats) + tuple(parts),
        cost=pl.CostEstimate(flops=20_000_000_000, bytes_accessed=0, transcendentals=0),
    )
    m_inner, m_outer = swaps(msg)
    m_partner = to_partner(msg)
    out, d_queries = call(
        query_kernel,
        "query_gradient",
        (wide(rows, BF16),) * 2,
        (on, queries, gain, attn, msg, stats, lines, own, partner, inner, outer, fifth),
    )
    q_fifth = passed_on(q_inner, q_outer)
    m_inner, m_outer, m_partner, q_fifth, d_queries = lax.optimization_barrier(
        (m_inner, m_outer, m_partner, q_fifth, d_queries)
    )
    m_fifth = passed_on(m_inner, m_outer)
    dk_near, dv_near = call(
        functools.partial(near_key_kernel, spacing),
        "near_key_gradient",
        (wide(rows),) * 2,
        (own, queries, q_partner, q_inner, q_outer, msg, m_partner, m_inner, m_outer),
    )
    d_keys, d_values = call(
        functools.partial(far_key_kernel, spacing),
        "far_key_gradient",
        (wide(rows, BF16),) * 2,
        (own, dk_near, dv_near, q_fifth, m_fifth),
    )
    return out, d_queries, d_keys, d_values


def solution(mesh):
    in_specs = (
        P("band", "head"),
        P("band", "head"),
        P("band", "head"),
        P("band", "head"),
        P("head"),
        P("band", None),
    )
    out_specs = (P("band", "head"), P("band", "head"), P("band", "head"), P("band", "head"))
    return jax.shard_map(local, mesh=mesh, in_specs=in_specs, out_specs=out_specs, check_vma=False)
```

time: 59.6 us -> 35.8 us (0.60)
  the two profiles are of different devices: /device:TPU:1 before, /device:TPU:5 now
where the time goes in v1:
time: 35.8 us; the launch traced here: 35.4 us
  starting transfers between devices  18.5 us (52%)
  waiting for transfers between devices  8.53 us (24%)
  Pallas kernels  5.87 us (16%)
  other arithmetic  1.07 us (3%)
  between operations  0.75 us (2%)
  local copies, waits for them, and re-layouts  0.7 us (2%)
    ppermute x4, starting transfers between devices, swaps(): lax.ppermute(array, 'band', pairs)  6.94 us
    ppermute x6, starting transfers between devices, to_partner(): return lax.ppermute(array, 'band', partner_pairs)  6.6 us
    pallas_call x6, Pallas kernels, call(): pl.pallas_call(kernel, name=name, out_shape=out_shape, in_specs=specs, ou...  5.87 us
    ppermute x4, waiting for transfers between devices, swaps(): lax.ppermute(array, 'band', pairs)  5.67 us
    ppermute x3, starting transfers between devices, head_sum_parts(): parts.append(lax.ppermute(sums, 'head', pairs))  3.67 us
    ppermute x3, waiting for transfers between devices, head_sum_parts(): parts.append(lax.ppermute(sums, 'head', pairs))  1.66 us
    ppermute x1, starting transfers between devices, local(): q_outer = lax.ppermute(q_relayed, 'band', relay_pairs)  1.28 us
    ppermute x6, waiting for transfers between devices, to_partner(): return lax.ppermute(array, 'band', partner_pairs)  1.19 us
  transfers between devices with their start and end apart: 15, of which 5 were waited for; matrix products, arithmetic and copies ran while one was open for 0% of the time, Pallas kernels for 13%

profile of v1, /device:TPU:5, one launch (start us, length us, event | category | flops | bytes accessed | tf_op | source)
XLA Modules:
  0.0 35.4 jit_solution(3195701254365112062)
XLA Ops:
  0.7 1.0 %pad_maximum_fusion.own = bf16[2,128,384]{2,1,0:T(8,128)(2,1)S(1)} fusion(bf16[1,128,384]{2,1,0:T(8,128)(2,1)} %bitcast.2, bf16[1,128,384]{2,1,0:T(8,128)(2,1)} %bitcast.3), kind=kLoop, calls=%fused_computation | loop fusion | flops 98304 | bytes 393216 | tf_op jit(solution)/shard_map/stack | solution.py:320
  1.7 1.3 %collective-permute-start = (bf16[2,128,384]{2,1,0:T(8,128)(2,1)S(1)}, bf16[2,128,384]{2,1,0:T(8,128)(2,1)S(1)}, u32[]{:S(2)}, u32[]{:S(2)}) collective-permute-start(bf16[2,128,384]{2,1,0:T(8,128)(2,1)S(1)} %pad_maximum_fusion.own), channel_id=1, source_target_pairs={{0,8},{4,12},{8,0},{12,4},{16,24},{20,28},{24,16},{28,20},{1,9},{5... | collective-permute-start | bytes 589832 | tf_op jit(solution)/shard_map/ppermute | solution.py:315
  2.9 1.0 %collective-permute-start.1 = (bf16[2,128,384]{2,1,0:T(8,128)(2,1)S(1)}, bf16[2,128,384]{2,1,0:T(8,128)(2,1)S(1)}, u32[]{:S(2)}, u32[]{:S(2)}) collective-permute-start(bf16[2,128,384]{2,1,0:T(8,128)(2,1)S(1)} %pad_maximum_fusion.own), channel_id=1, source_target_pairs={{0,4},{4,0},{8,12},{12,8},{16,20},{20,16},{24,28},{28,24},{1,5},{5... | collective-permute-start | bytes 589832 | tf_op jit(solution)/shard_map/ppermute | solution.py:312
  3.9 1.9 %collective-permute-start.3 = (bf16[2,128,384]{2,1,0:T(8,128)(2,1)S(1)}, bf16[2,128,384]{2,1,0:T(8,128)(2,1)S(1)}, u32[]{:S(2)}, u32[]{:S(2)}) collective-permute-start(bf16[2,128,384]{2,1,0:T(8,128)(2,1)S(1)} %pad_maximum_fusion.own), channel_id=1, source_target_pairs={{8,16},{12,20},{16,8},{20,12},{9,17},{13,21},{17,9},{21,13},{10,18... | collective-permute-start | bytes 589832 | tf_op jit(solution)/shard_map/ppermute | solution.py:315
  5.9 0.7 %copy-done.3 = f32[384]{0:T(512)S(1)} copy-done((f32[384]{0:T(512)S(1)}, f32[384]{0:T(512)}, u32[]{:S(2)}) %copy-start.3) | copy-done | bytes 1560
  6.6 0.9 %collective-permute-done.inner = bf16[2,128,384]{2,1,0:T(8,128)(2,1)S(1)} collective-permute-done((bf16[2,128,384]{2,1,0:T(8,128)(2,1)S(1)}, bf16[2,128,384]{2,1,0:T(8,128)(2,1)S(1)}, u32[]{:S(2)}, u32[]{:S(2)}) %collective-permute-start) | collective-permute-done | bytes 196640 | tf_op jit(solution)/shard_map/ppermute | solution.py:315
  7.5 0.9 %near_attention.1 = (f32[1152,128]{1,0:T(8,128)S(1)}, f32[8,128]{1,0:T(8,128)S(1)}, f32[384,128]{1,0:T(8,128)S(1)}, f32[8,128]{1,0:T(8,128)S(1)}) custom-call(s32[1,4]{1,0:T(1,128)S(1)} %copy-done.2, bf16[128,384]{1,0:T(8,128)(2,1)S(1)} %copy-done, bf16[128,384]{1,0:T(8,128)(2,1)S(1)} %copy-done.1, f32[1,384]{1,0:T(1,128)S(1)} %broadcast_in_dim.3.gain_ref, ...), custom_call_target="tpu_custom_call" | custom-call | tf_op jit(solution)/shard_map/near_attention/pallas_call | solution.py:256
  8.4 4.8 %collective-permute-done.3.outer = bf16[2,128,384]{2,1,0:T(8,128)(2,1)S(1)} collective-permute-done((bf16[2,128,384]{2,1,0:T(8,128)(2,1)S(1)}, bf16[2,128,384]{2,1,0:T(8,128)(2,1)S(1)}, u32[]{:S(2)}, u32[]{:S(2)}) %collective-permute-start.3) | collective-permute-done | bytes 196640 | tf_op jit(solution)/shard_map/ppermute | solution.py:315
  13.2 0.8 %collective-permute-start.4 = (bf16[2,128,384]{2,1,0:T(8,128)(2,1)S(1)}, bf16[2,128,384]{2,1,0:T(8,128)(2,1)S(1)}, u32[]{:S(2)}, u32[]{:S(2)}) collective-permute-start(bf16[2,128,384]{2,1,0:T(8,128)(2,1)S(1)} %broadcast_select_fusion), channel_id=1, source_target_pairs={{0,4},{4,0},{8,12},{12,8},{16,20},{20,16},{24,28},{28,24},{1,5},{5... | collective-permute-start | bytes 589832 | tf_op jit(solution)/shard_map/ppermute | solution.py:312
  14.1 1.1 %collective-permute-done.4.fifth = bf16[2,128,384]{2,1,0:T(8,128)(2,1)S(1)} collective-permute-done((bf16[2,128,384]{2,1,0:T(8,128)(2,1)S(1)}, bf16[2,128,384]{2,1,0:T(8,128)(2,1)S(1)}, u32[]{:S(2)}, u32[]{:S(2)}) %collective-permute-start.4) | collective-permute-done | bytes 196640 | tf_op jit(solution)/shard_map/ppermute | solution.py:312
  15.2 1.1 %far_attention.1 = (bf16[384,128]{1,0:T(8,128)(2,1)S(1)}, f32[8,128]{1,0:T(8,128)S(1)}, f32[8,128]{1,0:T(8,128)S(1)}) custom-call(bf16[128,384]{1,0:T(8,128)(2,1)S(1)} %copy-done, f32[384,128]{1,0:T(8,128)S(1)} %get-tuple-element.37.grad_ref.refs_2_, f32[1152,128]{1,0:T(8,128)S(1)} %get-tuple-element.40.exps_ref, f32[8,128]{1,0:T(8,128)S(1)} %get-tuple-element.41.near_ref, ...), custom_call_target="tpu_custom_call" | custom-call | tf_op jit(solution)/shard_map/far_attention/pallas_call | solution.py:256
  16.2 2.4 %collective-permute-start.6 = (f32[8,128]{1,0:T(8,128)S(1)}, f32[8,128]{1,0:T(8,128)S(1)}, u32[]{:S(2)}, u32[]{:S(2)}) collective-permute-start(f32[8,128]{1,0:T(8,128)S(1)} %get-tuple-element.48.refs_4_), channel_id=1, source_target_pairs={{0,2},{1,3},{2,0},{3,1},{4,6},{5,7},{6,4},{7,5},{8,10},{9,11},{10,... | collective-permute-start | bytes 12296 | tf_op jit(solution)/shard_map/ppermute | solution.py:290
  18.6 1.1 %collective-permute-start.7 = (f32[8,128]{1,0:T(8,128)S(1)}, f32[8,128]{1,0:T(8,128)S(1)}, u32[]{:S(2)}, u32[]{:S(2)}) collective-permute-start(f32[8,128]{1,0:T(8,128)S(1)} %get-tuple-element.48.refs_4_), channel_id=1, source_target_pairs={{0,3},{1,2},{2,1},{3,0},{4,7},{5,6},{6,5},{7,4},{8,11},{9,10},{10,... | collective-permute-start | bytes 12296 | tf_op jit(solution)/shard_map/ppermute | solution.py:290
  19.7 0.2 collective-permute-start.8
  19.9 1.3 %collective-permute-start.12 = (bf16[128,384]{1,0:T(8,128)(2,1)S(1)}, bf16[128,384]{1,0:T(8,128)(2,1)S(1)}, u32[]{:S(2)}, u32[]{:S(2)}) collective-permute-start(bf16[128,384]{1,0:T(8,128)(2,1)S(1)} %collective-permute-done.5.q2), channel_id=1, source_target_pairs={{0,16},{4,20},{24,8},{28,12},{1,17},{5,21},{25,9},{29,13},{2,18},{... | collective-permute-start | bytes 294920 | tf_op jit(solution)/shard_map/ppermute | solution.py:342
  21.2 1.7 %collective-permute-done.7.refs_6_ = f32[8,128]{1,0:T(8,128)S(1)} collective-permute-done((f32[8,128]{1,0:T(8,128)S(1)}, f32[8,128]{1,0:T(8,128)S(1)}, u32[]{:S(2)}, u32[]{:S(2)}) %collective-permute-start.7) | collective-permute-done | bytes 4128 | tf_op jit(solution)/shard_map/ppermute | solution.py:290
  23.0 0.7 %collective-permute-start.9 = (bf16[432,128]{1,0:T(8,128)(2,1)S(1)}, bf16[432,128]{1,0:T(8,128)(2,1)S(1)}, u32[]{:S(2)}, u32[]{:S(2)}) collective-permute-start(bf16[432,128]{1,0:T(8,128)(2,1)S(1)} %get-tuple-element.52.msg_ref.m0), channel_id=1, source_target_pairs={{0,8},{4,12},{8,0},{12,4},{16,24},{20,28},{24,16},{28,20},{1,9},{5... | collective-permute-start | bytes 331784 | tf_op jit(solution)/shard_map/ppermute | solution.py:315
  23.7 3.0 %collective-permute-start.10 = (bf16[432,128]{1,0:T(8,128)(2,1)S(1)}, bf16[432,128]{1,0:T(8,128)(2,1)S(1)}, u32[]{:S(2)}, u32[]{:S(2)}) collective-permute-start(bf16[432,128]{1,0:T(8,128)(2,1)S(1)} %get-tuple-element.52.msg_ref.m0), channel_id=1, source_target_pairs={{8,16},{12,20},{16,8},{20,12},{9,17},{13,21},{17,9},{21,13},{10,18... | collective-permute-start | bytes 331784 | tf_op jit(solution)/shard_map/ppermute | solution.py:315
  26.7 2.4 %collective-permute-start.11 = (bf16[432,128]{1,0:T(8,128)(2,1)S(1)}, bf16[432,128]{1,0:T(8,128)(2,1)S(1)}, u32[]{:S(2)}, u32[]{:S(2)}) collective-permute-start(bf16[432,128]{1,0:T(8,128)(2,1)S(1)} %get-tuple-element.52.msg_ref.m0), channel_id=1, source_target_pairs={{0,4},{4,0},{8,12},{12,8},{16,20},{20,16},{24,28},{28,24},{1,5},{5... | collective-permute-start | bytes 331784 | tf_op jit(solution)/shard_map/ppermute | solution.py:312
  29.2 1.6 %query_gradient.1 = (bf16[128,384]{1,0:T(8,128)(2,1)}, bf16[128,384]{1,0:T(8,128)(2,1)}) custom-call(f32[8,128]{1,0:T(8,128)S(1)} %get-tuple-element.36.on_ref.refs_0_, bf16[128,384]{1,0:T(8,128)(2,1)S(1)} %copy-done, f32[1,384]{1,0:T(1,128)S(1)} %broadcast_in_dim.3.gain_ref, bf16[384,128]{1,0:T(8,128)(2,1)S(1)} %get-tuple-element.45.refs_1_.attn_ref, ...), custom_call_target="tpu_custom_call" | custom-call | tf_op jit(solution)/shard_map/query_gradient/pallas_call | solution.py:256
  30.9 2.2 %collective-permute-start.14 = (bf16[432,128]{1,0:T(8,128)(2,1)S(1)}, bf16[432,128]{1,0:T(8,128)(2,1)S(1)}, u32[]{:S(2)}, u32[]{:S(2)}) collective-permute-start(bf16[432,128]{1,0:T(8,128)(2,1)S(1)} %broadcast_select_fusion.1), channel_id=1, source_target_pairs={{0,4},{4,0},{8,12},{12,8},{16,20},{20,16},{24,28},{28,24},{1,5},{5... | collective-permute-start | bytes 331784 | tf_op jit(solution)/shard_map/ppermute | solution.py:312
  33.1 0.8 %near_key_gradient.1 = (f32[128,384]{1,0:T(8,128)S(1)}, f32[128,384]{1,0:T(8,128)S(1)}) custom-call(bf16[2,128,384]{2,1,0:T(8,128)(2,1)S(1)} %pad_maximum_fusion.own, bf16[128,384]{1,0:T(8,128)(2,1)S(1)} %copy-done, bf16[128,384]{1,0:T(8,128)(2,1)S(1)} %collective-permute-done.2.q1, bf16[128,384]{1,0:T(8,128)(2,1)S(1)} %collective-permute-done.5.q2, ...), custom_call_target="tpu_custom_call" | custom-call | tf_op jit(solution)/shard_map/near_key_gradient/pallas_call | solution.py:256
  34.0 0.1 collective-permute-done.14.m4
  34.1 1.3 %far_key_gradient.1 = (bf16[128,384]{1,0:T(8,128)(2,1)}, bf16[128,384]{1,0:T(8,128)(2,1)}) custom-call(bf16[2,128,384]{2,1,0:T(8,128)(2,1)S(1)} %pad_maximum_fusion.own, f32[128,384]{1,0:T(8,128)S(1)} %get-tuple-element.63.dk_near, f32[128,384]{1,0:T(8,128)S(1)} %get-tuple-element.64.dv_near, bf16[128,384]{1,0:T(8,128)(2,1)S(1)} %collective-permute-done.13.q4, ...), custom_call_target="tpu_custom_call" | custom-call | tf_op jit(solution)/shard_map/far_key_gradient/pallas_call | solution.py:256
  (25 shorter events, 0.4 us)
Async XLA Ops:
  0.6 5.2 %copy-start = (bf16[128,384]{1,0:T(8,128)(2,1)S(1)}, bf16[128,384]{1,0:T(8,128)(2,1)}, u32[]{:S(2)}) copy-start(bf16[128,384]{1,0:T(8,128)(2,1)} %q0.1) | copy-start | bytes 294916
  0.6 6.9 %copy-start.1 = (bf16[128,384]{1,0:T(8,128)(2,1)S(1)}, bf16[128,384]{1,0:T(8,128)(2,1)}, u32[]{:S(2)}) copy-start(bf16[128,384]{1,0:T(8,128)(2,1)} %g_ref.1) | copy-start | bytes 294916
  1.7 5.8 %collective-permute-start = (bf16[2,128,384]{2,1,0:T(8,128)(2,1)S(1)}, bf16[2,128,384]{2,1,0:T(8,128)(2,1)S(1)}, u32[]{:S(2)}, u32[]{:S(2)}) collective-permute-start(bf16[2,128,384]{2,1,0:T(8,128)(2,1)S(1)} %pad_maximum_fusion.own), channel_id=1, source_target_pairs={{0,8},{4,12},{8,0},{12,4},{16,24},{20,28},{24,16},{28,20},{1,9},{5... | collective-permute-start | bytes 589832 | tf_op jit(solution)/shard_map/ppermute | solution.py:315
  2.9 4.6 %collective-permute-start.1 = (bf16[2,128,384]{2,1,0:T(8,128)(2,1)S(1)}, bf16[2,128,384]{2,1,0:T(8,128)(2,1)S(1)}, u32[]{:S(2)}, u32[]{:S(2)}) collective-permute-start(bf16[2,128,384]{2,1,0:T(8,128)(2,1)S(1)} %pad_maximum_fusion.own), channel_id=1, source_target_pairs={{0,4},{4,0},{8,12},{12,8},{16,20},{20,16},{24,28},{28,24},{1,5},{5... | collective-permute-start | bytes 589832 | tf_op jit(solution)/shard_map/ppermute | solution.py:312
  3.9 9.3 %collective-permute-start.3 = (bf16[2,128,384]{2,1,0:T(8,128)(2,1)S(1)}, bf16[2,128,384]{2,1,0:T(8,128)(2,1)S(1)}, u32[]{:S(2)}, u32[]{:S(2)}) collective-permute-start(bf16[2,128,384]{2,1,0:T(8,128)(2,1)S(1)} %pad_maximum_fusion.own), channel_id=1, source_target_pairs={{8,16},{12,20},{16,8},{20,12},{9,17},{13,21},{17,9},{21,13},{10,18... | collective-permute-start | bytes 589832 | tf_op jit(solution)/shard_map/ppermute | solution.py:315
  5.8 2.6 %collective-permute-start.2 = (bf16[128,384]{1,0:T(8,128)(2,1)S(1)}, bf16[128,384]{1,0:T(8,128)(2,1)S(1)}, u32[]{:S(2)}, u32[]{:S(2)}) collective-permute-start(bf16[128,384]{1,0:T(8,128)(2,1)S(1)} %copy-done), channel_id=1, source_target_pairs={{0,4},{4,0},{8,12},{12,8},{16,20},{20,16},{24,28},{28,24},{1,5},{5... | collective-permute-start | bytes 294920 | tf_op jit(solution)/shard_map/ppermute | solution.py:312
  5.9 0.7 %copy-start.3 = (f32[384]{0:T(512)S(1)}, f32[384]{0:T(512)}, u32[]{:S(2)}) copy-start(f32[384]{0:T(512)} %param.10) | copy-start | bytes 4612
  6.6 0.9 %copy-start.2 = (s32[1,4]{1,0:T(1,128)S(1)}, s32[1,4]{1,0:T(1,128)}, u32[]{:S(2)}) copy-start(s32[1,4]{1,0:T(1,128)} %flags_ref.1) | copy-start | bytes 52
  13.2 1.9 %collective-permute-start.4 = (bf16[2,128,384]{2,1,0:T(8,128)(2,1)S(1)}, bf16[2,128,384]{2,1,0:T(8,128)(2,1)S(1)}, u32[]{:S(2)}, u32[]{:S(2)}) collective-permute-start(bf16[2,128,384]{2,1,0:T(8,128)(2,1)S(1)} %broadcast_select_fusion), channel_id=1, source_target_pairs={{0,4},{4,0},{8,12},{12,8},{16,20},{20,16},{24,28},{28,24},{1,5},{5... | collective-permute-start | bytes 589832 | tf_op jit(solution)/shard_map/ppermute | solution.py:312
  14.1 5.8 %collective-permute-start.5 = (bf16[128,384]{1,0:T(8,128)(2,1)S(1)}, bf16[128,384]{1,0:T(8,128)(2,1)S(1)}, u32[]{:S(2)}, u32[]{:S(2)}) collective-permute-start(bf16[128,384]{1,0:T(8,128)(2,1)S(1)} %copy-done), channel_id=1, source_target_pairs={{0,8},{4,12},{8,0},{12,4},{16,24},{20,28},{24,16},{28,20},{1,9},{5... | collective-permute-start | bytes 294920 | tf_op jit(solution)/shard_map/ppermute | solution.py:334
  16.2 5.0 %collective-permute-start.6 = (f32[8,128]{1,0:T(8,128)S(1)}, f32[8,128]{1,0:T(8,128)S(1)}, u32[]{:S(2)}, u32[]{:S(2)}) collective-permute-start(f32[8,128]{1,0:T(8,128)S(1)} %get-tuple-element.48.refs_4_), channel_id=1, source_target_pairs={{0,2},{1,3},{2,0},{3,1},{4,6},{5,7},{6,4},{7,5},{8,10},{9,11},{10,... | collective-permute-start | bytes 12296 | tf_op jit(solution)/shard_map/ppermute | solution.py:290
  18.6 4.3 %collective-permute-start.7 = (f32[8,128]{1,0:T(8,128)S(1)}, f32[8,128]{1,0:T(8,128)S(1)}, u32[]{:S(2)}, u32[]{:S(2)}) collective-permute-start(f32[8,128]{1,0:T(8,128)S(1)} %get-tuple-element.48.refs_4_), channel_id=1, source_target_pairs={{0,3},{1,2},{2,1},{3,0},{4,7},{5,6},{6,5},{7,4},{8,11},{9,10},{10,... | collective-permute-start | bytes 12296 | tf_op jit(solution)/shard_map/ppermute | solution.py:290
  19.7 3.2 %collective-permute-start.8 = (f32[8,128]{1,0:T(8,128)S(1)}, f32[8,128]{1,0:T(8,128)S(1)}, u32[]{:S(2)}, u32[]{:S(2)}) collective-permute-start(f32[8,128]{1,0:T(8,128)S(1)} %get-tuple-element.48.refs_4_), channel_id=1, source_target_pairs={{0,1},{1,0},{2,3},{3,2},{4,5},{5,4},{6,7},{7,6},{8,9},{9,8},{10,11... | collective-permute-start | bytes 12296 | tf_op jit(solution)/shard_map/ppermute | solution.py:290
  19.9 9.2 %collective-permute-start.12 = (bf16[128,384]{1,0:T(8,128)(2,1)S(1)}, bf16[128,384]{1,0:T(8,128)(2,1)S(1)}, u32[]{:S(2)}, u32[]{:S(2)}) collective-permute-start(bf16[128,384]{1,0:T(8,128)(2,1)S(1)} %collective-permute-done.5.q2), channel_id=1, source_target_pairs={{0,16},{4,20},{24,8},{28,12},{1,17},{5,21},{25,9},{29,13},{2,18},{... | collective-permute-start | bytes 294920 | tf_op jit(solution)/shard_map/ppermute | solution.py:342
  23.0 7.9 %collective-permute-start.9 = (bf16[432,128]{1,0:T(8,128)(2,1)S(1)}, bf16[432,128]{1,0:T(8,128)(2,1)S(1)}, u32[]{:S(2)}, u32[]{:S(2)}) collective-permute-start(bf16[432,128]{1,0:T(8,128)(2,1)S(1)} %get-tuple-element.52.msg_ref.m0), channel_id=1, source_target_pairs={{0,8},{4,12},{8,0},{12,4},{16,24},{20,28},{24,16},{28,20},{1,9},{5... | collective-permute-start | bytes 331784 | tf_op jit(solution)/shard_map/ppermute | solution.py:315
  23.7 7.2 %collective-permute-start.10 = (bf16[432,128]{1,0:T(8,128)(2,1)S(1)}, bf16[432,128]{1,0:T(8,128)(2,1)S(1)}, u32[]{:S(2)}, u32[]{:S(2)}) collective-permute-start(bf16[432,128]{1,0:T(8,128)(2,1)S(1)} %get-tuple-element.52.msg_ref.m0), channel_id=1, source_target_pairs={{8,16},{12,20},{16,8},{20,12},{9,17},{13,21},{17,9},{21,13},{10,18... | collective-permute-start | bytes 331784 | tf_op jit(solution)/shard_map/ppermute | solution.py:315
  26.7 4.2 %collective-permute-start.11 = (bf16[432,128]{1,0:T(8,128)(2,1)S(1)}, bf16[432,128]{1,0:T(8,128)(2,1)S(1)}, u32[]{:S(2)}, u32[]{:S(2)}) collective-permute-start(bf16[432,128]{1,0:T(8,128)(2,1)S(1)} %get-tuple-element.52.msg_ref.m0), channel_id=1, source_target_pairs={{0,4},{4,0},{8,12},{12,8},{16,20},{20,16},{24,28},{28,24},{1,5},{5... | collective-permute-start | bytes 331784 | tf_op jit(solution)/shard_map/ppermute | solution.py:312
  29.1 1.7 %collective-permute-start.13 = (bf16[128,384]{1,0:T(8,128)(2,1)S(1)}, bf16[128,384]{1,0:T(8,128)(2,1)S(1)}, u32[]{:S(2)}, u32[]{:S(2)}) collective-permute-start(bf16[128,384]{1,0:T(8,128)(2,1)S(1)} %broadcast_select_fusion.2), channel_id=1, source_target_pairs={{0,4},{4,0},{8,12},{12,8},{16,20},{20,16},{24,28},{28,24},{1,5},{5... | collective-permute-start | bytes 294920 | tf_op jit(solution)/shard_map/ppermute | solution.py:312
  30.9 3.2 %collective-permute-start.14 = (bf16[432,128]{1,0:T(8,128)(2,1)S(1)}, bf16[432,128]{1,0:T(8,128)(2,1)S(1)}, u32[]{:S(2)}, u32[]{:S(2)}) collective-permute-start(bf16[432,128]{1,0:T(8,128)(2,1)S(1)} %broadcast_select_fusion.1), channel_id=1, source_target_pairs={{0,4},{4,0},{8,12},{12,8},{16,20},{20,16},{24,28},{28,24},{1,5},{5... | collective-permute-start | bytes 331784 | tf_op jit(solution)/shard_map/ppermute | solution.py:312
